TPU v7x, 256 devices: a whole 4x4x8 slice. The times are simulated.
256 devices in a mesh: dp: 64 (over y, z, core), tensor: 4 (over x).
Axes of the slice: x: 4, y: 4, z: 8, core: 2. Of those that a mesh axis runs over, the one named last changes fastest.
Arguments:
- acts: bfloat16 [65536, 1280], P('dp'), may hold values from -24 to 24, as said below
- cotangent: bfloat16 [65536, 5120], P('dp', 'tensor'), may hold values from -0.1875 to 0.1875
- error_prev: bfloat16 [81920, 5120], P('dp', 'tensor'), may hold values from -3 to 3
- q_prev: bfloat16 [64, 5120], P(None, 'tensor'), may hold values from -0.078125 to 0.078125
Outputs:
- error_new: bfloat16 [81920, 5120], P('dp', 'tensor')
- q_new: float32 [64, 5120], P(None, 'tensor')
Inputs may be any that keep to these rules, and one draw needn't show every extreme that they name: `acts`: entries of the layer's inputs.
All inputs are finite; a program needn't handle non-finite values.
Results may differ from a plain program's by a relative error of at most 0.0058.
Values may be sent and summed in bfloat16 or wider, within the bound.
A program may use at most 64 MiB of HBM per device.

v0:
```python
import jax
import jax.numpy as jnp
from jax import lax
from jax.sharding import PartitionSpec as P


def orthonormal(rows_part, gram_matrix):
    lower_factor = jnp.linalg.cholesky(gram_matrix)
    return jax.scipy.linalg.solve_triangular(lower_factor, rows_part.T, lower=True).T.astype(
        jnp.bfloat16
    )


def self_gram(matrix):
    return jnp.dot(
        matrix.T, matrix, precision=lax.Precision.HIGHEST, preferred_element_type=jnp.float32
    )


def body(acts, cotangent, error_prev, q_prev):
    replicas = lax.axis_size("dp")
    gradient = lax.dot_general(
        acts, cotangent, (((0,), (0,)), ((), ())), preferred_element_type=jnp.float32
    )
    merged = (gradient + error_prev.astype(jnp.float32)).astype(jnp.bfloat16)
    partial_left = lax.dot_general(
        merged, q_prev, (((1,), (1,)), ((), ())), preferred_element_type=jnp.float32
    )
    project = lax.psum(partial_left, ("dp", "tensor"))
    basis = orthonormal(project, self_gram(project))
    fold_term = lax.dot_general(
        basis, merged, (((0,), (0,)), ((), ())), preferred_element_type=jnp.float32
    )
    q_new = lax.psum(fold_term, "dp") / replicas
    low_rank = jnp.dot(basis, q_new.astype(jnp.bfloat16), preferred_element_type=jnp.float32)
    error_new = (merged.astype(jnp.float32) - low_rank).astype(jnp.bfloat16)
    return (error_new, q_new)


def solution(mesh):
    return jax.shard_map(
        body,
        mesh=mesh,
        in_specs=(P("dp", None), P("dp", "tensor"), P("dp", "tensor"), P(None, "tensor")),
        out_specs=(P("dp", "tensor"), P(None, "tensor")),
        check_vma=False,
    )
```

profile of v0, /device:TPU:1, one launch (start us, length us, event | category | flops | bytes accessed | tf_op | source)
XLA Modules:
  0.0 475.0 jit_solution(3146195647857923316)
XLA Ops:
  7.2 0.0 copy-start
  7.2 0.0 copy-start.3
  7.2 0.0 all-reduce.3.cloned.1.call-start
  7.2 1.7 copy-done
  8.9 6.1 %fusion.1 = bf16[1280,1280]{1,0:T(8,128)(2,1)S(1)} fusion(bf16[1024,1280]{1,0:T(8,128)(2,1)S(1)} %copy-done, bf16[1024,1280]{1,0:T(8,128)(2,1)} %param.5, bf16[1280,1280]{1,0:T(8,128)(2,1)} %param.6), kind=kOutput, calls=%fused_computation.3 | convolution fusion | flops 3360358400 | bytes 11796480 | tf_op jit(solution)/shard_map/dot_general | solution.py:22
  15.0 0.0 copy-start.1
  15.0 1.7 copy-done.1
  16.7 0.0 copy-done.3
  16.7 1.9 fusion.6
  18.6 0.0 all-reduce.3.cloned.1.call-update
  18.6 0.0 all-reduce.5.cloned.1.call-start
  18.7 249.9 %all-reduce.3.cloned.1.call-done = f32[1280,64]{0,1:T(8,128)} async-done(((f32[1280,64]{0,1:T(8,128)}), f32[1280,64]{0,1:T(8,128)}) %all-reduce.3.cloned.1.call-update) | async-done | bytes 327696 | tf_op jit(solution)/shard_map/psum | solution.py:29
  268.5 1.5 fusion.7
  270.0 0.1 copy.6
  270.1 5.8 %cholesky.16 = f32[64,64]{1,0:T(8,128)S(1)} custom-call(f32[64,64]{1,0:T(8,128)S(1)} %fusion.5), custom_call_target="Cholesky" | custom-call | tf_op jit(solution)/shard_map/jit(cholesky)/cholesky | solution.py:8
  276.0 0.6 compare_reduce_fusion
  276.6 0.7 fusion.3
  277.3 4.9 %custom-call.7 = f32[1,64,64]{1,2,0:T(8,128)S(1)} custom-call(f32[1,64,64]{2,1,0:T(8,128)S(1)} %fusion.3), custom_call_target="InvertDiagBlocksLowerTriangular" | custom-call | tf_op jit(solution)/shard_map/jit(_solve_triangular)/triangular_solve | solution.py:9
  282.2 1.5 convolution_convert_fusion
  283.6 3.4 fusion.8
  287.0 0.0 all-reduce.5.cloned.1.call-update
  287.0 175.3 %all-reduce.5.cloned.1.call-done = f32[64,1280]{1,0:T(8,128)} async-done(((f32[64,1280]{1,0:T(8,128)}), f32[64,1280]{1,0:T(8,128)}) %all-reduce.5.cloned.1.call-update) | async-done | bytes 327696 | tf_op jit(solution)/shard_map/psum | solution.py:34
  462.3 1.0 broadcast_multiply_fusion
  463.3 0.0 copy-start.2
  463.3 4.8 %fusion = bf16[1280,1280]{1,0:T(8,128)(2,1)} fusion(bf16[1280,64]{0,1:T(8,128)(2,1)S(1)} %convolution_convert_fusion, bf16[1280,1280]{1,0:T(8,128)(2,1)} %copy-done.1, f32[64,1280]{1,0:T(8,128)S(1)} %broadcast_multiply_fusion), kind=kOutput, calls=%fused_computation.2 | convolution fusion | flops 214712320 | bytes 7045120 | tf_op jit(solution)/shard_map/dot_general | solution.py:35
  468.1 0.0 copy-done.2
  (2 shorter events, 0.0 us)
Async XLA Ops:
  7.2 1.7 copy-start
  7.2 9.6 %copy-start.3 = (bf16[64,1280]{1,0:T(8,128)(2,1)S(1)}, bf16[64,1280]{1,0:T(8,128)(2,1)}, u32[]{:S(2)}) copy-start(bf16[64,1280]{1,0:T(8,128)(2,1)} %param.7) | copy-start | bytes 491524
  7.2 261.3 %all-reduce.3.cloned.1.call-start = ((), (), s32[]{:S(2)}) async-start(), calls=%async_computation | async-start | bytes 655360 | tf_op jit(solution)/shard_map/psum | solution.py:29
  15.0 1.7 copy-start.1
  18.6 443.7 %all-reduce.5.cloned.1.call-start = ((), (), s32[]{:S(2)}) async-start(), calls=%async_computation.1 | async-start | bytes 655360 | tf_op jit(solution)/shard_map/psum | solution.py:34
  463.3 4.8 %copy-start.2 = (f32[64,1280]{1,0:T(8,128)}, f32[64,1280]{1,0:T(8,128)S(1)}, u32[]{:S(2)}) copy-start(f32[64,1280]{1,0:T(8,128)S(1)} %broadcast_multiply_fusion) | copy-start | bytes 983044
Sparse Core Ops, SparseCore 0:
  18.7 249.7 all-reduce.2
  287.1 175.1 all-reduce.4
where the time goes:
time: 475 us
  waiting for transfers between devices  425 us (89%)
  matrix products  19 us (4%)
  between operations  14.1 us (3%)
  other arithmetic  13.1 us (3%)
    psum x1, waiting for transfers between devices, body(): project = lax.psum(partial_left, ('dp', 'tensor'))  250 us
    psum x1, waiting for transfers between devices, body(): q_new = lax.psum(fold_term, 'dp') / replicas  175 us
  transfers between devices with their start and end apart: 2, of which 2 were waited for; matrix products, arithmetic and copies ran while one was open for 0% of the time, Pallas kernels for 0%

commit v1 on v0

v1 whole, which is shorter than its diff:
```python
import functools

import jax
import jax.numpy as jnp
from jax import lax
from jax.experimental import pallas as pl
from jax.experimental.pallas import tpu as pltpu
from jax.sharding import PartitionSpec as P

ROWS = 1280
COLS = 1280
TOK = 1024
RANK = 64
REPLICAS = 64
NX, NY, NZ = 4, 4, 8
HALF = 640
F32 = jnp.float32
BF16 = jnp.bfloat16
ROW_CHUNKS = ((0, 256), (256, 384))
COL_CHUNKS = ((0, 256), (256, 256), (512, 256), (768, 256), (1024, 256))


def device(x, y, z, c):
    return {"dp": (y * NZ + z) * 2 + c, "tensor": x}


def send(src, dst, send_sem, recv_sem, target):
    pltpu.make_async_remote_copy(
        src_ref=src, dst_ref=dst, send_sem=send_sem, recv_sem=recv_sem,
        device_id=target, device_id_type=pl.DeviceIdType.MESH,
    ).start()


def wait_bytes(ref, sem):
    pltpu.make_async_copy(ref, ref, sem).wait()


def hops(d, n):
    return min(d, n - d)


XY = sorted(
    [(dx, dy) for dx in range(NX) for dy in range(NY) if (dx, dy) != (0, 0)],
    key=lambda d: -(hops(d[0], NX) + hops(d[1], NY)),
)
ZS = sorted(range(1, NZ), key=lambda d: -hops(d, NZ))


def slot_xy(dx, dy):
    return dx * NY + dy - 1


def eliminate(first, last, work):
    lane = lax.broadcasted_iota(jnp.int32, (RANK, 2 * RANK), 1)
    row = lax.broadcasted_iota(jnp.int32, (RANK, 2 * RANK), 0)

    def step(k, w):
        pivot_row = jnp.sum(jnp.where(row == k, w, 0.0), axis=0, keepdims=True)
        column = jnp.sum(jnp.where(lane == k, w, 0.0), axis=1, keepdims=True)
        pivot = jnp.sum(
            jnp.where(lane[:1] == k, pivot_row, 0.0), axis=1, keepdims=True
        )
        factor = column / pivot
        return w - jnp.where(row > k, factor * pivot_row, 0.0)

    return lax.fori_loop(first, last, step, work)


def sum_kernel(
    acts, cot, err, q_ref,
    merged_out, fold_out, inv_out, basis_out,
    acts_v, cot_v, err_v, q_v, at_v, merged, part,
    r1, s1, c1, u1, z1, g1, d1, proj, work,
    fb, fr, fs, z2,
    in_sem, out_sem, send_sem, recv_sem,
):
    dp = lax.axis_index("dp")
    x = lax.axis_index("tensor")
    c = lax.rem(dp, 2)
    z = lax.rem(dp // 2, NZ)
    y = dp // (2 * NZ)
    other = 1 - c

    def xy_peer(dx, dy):
        return device(lax.rem(x + dx, NX), lax.rem(y + dy, NY), z, c)

    def z_peer(dz):
        return device(x, y, lax.rem(z + dz, NZ), c)

    sibling = device(x, y, z, other)

    first_half = lax.rem(y, 2)
    loads = {}
    count = [0]

    def load(key, src, dst):
        copy = pltpu.make_async_copy(src, dst, in_sem.at[count[0]])
        count[0] += 1
        copy.start()
        loads[key] = copy

    def load_rows(s, j):
        half = lax.rem(first_half + s, 2)
        off, size = ROW_CHUNKS[j]
        start = pl.multiple_of(half * HALF + off, 128)
        load(("a", s, j), acts.at[:, pl.ds(start, size)], acts_v.at[:, pl.ds(s * HALF + off, size)])
        return start, size

    def load_err(s, j):
        half = lax.rem(first_half + s, 2)
        off, size = ROW_CHUNKS[j]
        start = pl.multiple_of(half * HALF + off, 128)
        load(("e", s, j), err.at[pl.ds(start, size), :], err_v.at[pl.ds(s * HALF + off, size), :])

    load_rows(0, 0)
    for n, (off, size) in enumerate(COL_CHUNKS):
        load(("c", n), cot.at[:, pl.ds(off, size)], cot_v.at[:, pl.ds(off, size)])
        if n == 0:
            load_err(0, 0)
    load("q", q_ref, q_v)
    load_rows(0, 1)
    load_err(0, 1)
    for j in range(2):
        load_rows(1, j)
        load_err(1, j)

    barrier = pltpu.get_barrier_semaphore()

    def greet(target):
        pl.semaphore_signal(barrier, inc=1, device_id=target, device_id_type=pl.DeviceIdType.MESH)

    for dx, dy in XY:
        greet(xy_peer(dx, dy))
    for dz in ZS:
        greet(z_peer(dz))
    greet(sibling)
    for dy in range(1, NY):
        greet(device(x, lax.rem(y + dy, NY), z, other))

    outs = []
    for s in range(2):
        half = lax.rem(first_half + s, 2)
        for j, (off, size) in enumerate(ROW_CHUNKS):
            start = pl.multiple_of(half * HALF + off, 128)
            loads[("a", s, j)].wait()
            at_v[:size, :] = acts_v[:, s * HALF + off : s * HALF + off + size].T
            if s == 0 and j == 0:
                loads[("c", 0)].wait()
            loads[("e", s, j)].wait()
            for n, (coff, csize) in enumerate(COL_CHUNKS):
                if s == 0 and j == 0 and n > 0:
                    loads[("c", n)].wait()
                grad = jnp.dot(
                    at_v[:size, :], cot_v[:, coff : coff + csize], preferred_element_type=F32
                )
                grad = grad + err_v[
                    s * HALF + off : s * HALF + off + size, coff : coff + csize
                ].astype(F32)
                merged[pl.ds(start, size), coff : coff + csize] = grad.astype(BF16)
            if s == 0 and j == 0:
                loads["q"].wait()
            part[s, :, off : off + size] = lax.dot_general(
                q_v[...], merged[pl.ds(start, size), :],
                (((1,), (1,)), ((), ())), preferred_element_type=F32,
            )
            out = pltpu.make_async_copy(
                merged.at[pl.ds(start, size), :], merged_out.at[pl.ds(start, size), :],
                out_sem.at[s * 2 + j],
            )
            out.start()
            outs.append(out)
        if s == 0:
            pl.semaphore_wait(barrier, len(XY) + len(ZS) + NY)
        for dx, dy in XY:
            if dy % 2 == s:
                tx, ty = lax.rem(x + dx, NX), lax.rem(y + dy, NY)
                block = pl.multiple_of((tx * 2 + ty // 2) * 8, 8)
                send(
                    part.at[s, pl.ds(block, 8), :], r1.at[slot_xy(dx, dy)],
                    send_sem.at[0], recv_sem.at[0], device(tx, ty, z, c),
                )

    mine = pl.multiple_of((x * 2 + y // 2) * 8, 8)
    wait_bytes(r1, recv_sem.at[0])
    total = part[0, pl.ds(mine, 8), :]
    for i in range(NX * NY - 1):
        total = total + r1[i]
    s1[...] = total
    send(s1, c1, send_sem.at[1], recv_sem.at[1], sibling)
    wait_bytes(c1, recv_sem.at[1])
    g1[...] = s1[...] + c1[...]
    own = pl.multiple_of(c * 256, 128)
    u1[...] = g1[:, pl.ds(own, 384)]
    for dz in ZS:
        send(u1, z1.at[z], send_sem.at[2], recv_sem.at[2], z_peer(dz))
    z1[z] = u1[...]
    wait_bytes(z1.at[pl.ds(0, NZ - 1)], recv_sem.at[2])
    total = z1[0]
    for i in range(1, NZ):
        total = total + z1[i]
    d1[:, pl.ds(own, 384)] = total
    give = pl.multiple_of(c * 384, 128)
    send(
        d1.at[:, pl.ds(give, 256)], d1.at[:, pl.ds(give, 256)],
        send_sem.at[3], recv_sem.at[3], sibling,
    )
    wait_bytes(d1.at[:, pl.ds(0, 256)], recv_sem.at[3])
    lanes = pl.ds(pl.multiple_of(lax.rem(y, 2) * HALF, 128), HALF)
    home = proj.at[pl.ds(mine, 8), lanes]
    for dx, dy in XY:
        send(d1, home, send_sem.at[4], recv_sem.at[4], xy_peer(dx, dy))
    proj[pl.ds(mine, 8), lanes] = d1[...]
    wait_bytes(r1, recv_sem.at[4])

    left = proj[...]
    high = left.astype(BF16)
    low = (left - high.astype(F32)).astype(BF16)
    stack = jnp.concatenate([high, low], axis=0)
    for h in range(2):
        both = jnp.dot(stack, merged[:, h * HALF : (h + 1) * HALF], preferred_element_type=F32)
        fb[:, h * HALF : (h + 1) * HALF] = (both[:RANK] + both[RANK:]).astype(BF16)
        for dy in (2, 1, 3, 0):
            ty = lax.rem(y + dy, NY)
            rows = pl.ds(pl.multiple_of(ty * 16, 16), 16)

            def give_fold():
                send(
                    fb.at[rows, pl.ds(h * HALF, HALF)], fr.at[y * 2 + c],
                    send_sem.at[5], recv_sem.at[5], device(x, ty, z, h),
                )

            if dy:
                give_fold()
            else:
                pl.when(c != h)(give_fold)
    fr[y * 2 + c] = fb[
        pl.ds(pl.multiple_of(y * 16, 16), 16), pl.ds(pl.multiple_of(c * HALF, 128), HALF)
    ]

    gram = lax.dot_general(
        left, left, (((1,), (1,)), ((), ())),
        precision=lax.Precision.HIGHEST, preferred_element_type=F32,
    )
    eye = (
        lax.broadcasted_iota(jnp.int32, (RANK, RANK), 0)
        == lax.broadcasted_iota(jnp.int32, (RANK, RANK), 1)
    ).astype(F32)
    work[...] = eliminate(0, 20, jnp.concatenate([gram, eye], axis=1))

    wait_bytes(fr.at[pl.ds(0, 2 * NY - 1)], recv_sem.at[5])
    total = fr[0].astype(F32)
    for i in range(1, 2 * NY):
        total = total + fr[i].astype(F32)
    z2[z] = total.astype(BF16)
    for dz in ZS:
        send(z2.at[z], z2.at[z], send_sem.at[6], recv_sem.at[6], z_peer(dz))
    work[...] = eliminate(20, RANK, work[...])
    wait_bytes(z2.at[pl.ds(0, NZ - 1)], recv_sem.at[6])
    total = z2[0].astype(F32)
    for i in range(1, NZ):
        total = total + z2[i].astype(F32)
    rows = pl.ds(pl.multiple_of(y * 16, 16), 16)
    lanes = pl.ds(pl.multiple_of(c * HALF, 128), HALF)
    fs[rows, lanes] = total.astype(BF16)
    for dy in (2, 1, 3):
        ty = lax.rem(y + dy, NY)
        for core in (other, c):
            send(
                fs.at[rows, lanes], fs.at[rows, lanes],
                send_sem.at[7], recv_sem.at[7], device(x, ty, z, core),
            )
    send(fs.at[rows, lanes], fs.at[rows, lanes], send_sem.at[7], recv_sem.at[7], sibling)

    eliminated = work[...]
    diagonal = jnp.sum(eliminated[:, :RANK] * eye, axis=1, keepdims=True)
    inverse = eliminated[:, RANK:] * lax.rsqrt(diagonal)
    inv_out[...] = inverse
    basis_out[...] = jnp.dot(
        inverse, proj[...], precision=lax.Precision.HIGHEST, preferred_element_type=F32
    ).astype(BF16)

    wait_bytes(fr.at[pl.ds(0, 2 * NY - 1)], recv_sem.at[7])
    fold_out[...] = fs[...]

    wait_bytes(r1, send_sem.at[0])
    wait_bytes(s1, send_sem.at[1])
    wait_bytes(z1.at[pl.ds(0, NZ - 1)], send_sem.at[2])
    wait_bytes(d1.at[:, pl.ds(0, 256)], send_sem.at[3])
    wait_bytes(r1, send_sem.at[4])
    wait_bytes(fr.at[pl.ds(0, 2 * NY - 1)], send_sem.at[5])
    wait_bytes(z2.at[pl.ds(0, NZ - 1)], send_sem.at[6])
    wait_bytes(fr.at[pl.ds(0, 2 * NY - 1)], send_sem.at[7])
    for out in outs:
        out.wait()


def update_kernel(merged, fold, inv, basis, error_new, q_new, q_low):
    @pl.when(pl.program_id(0) == 0)
    def _():
        q = jnp.dot(
            inv[...], fold[...].astype(F32),
            precision=lax.Precision.HIGHEST, preferred_element_type=F32,
        ) * (1.0 / REPLICAS)
        q_new[...] = q
        q_low[...] = q.astype(BF16)

    low_rank = lax.dot_general(
        basis[...], q_low[...], (((0,), (0,)), ((), ())), preferred_element_type=F32
    )
    error_new[...] = (merged[...].astype(F32) - low_rank).astype(BF16)


def body(acts, cotangent, error_prev, q_prev):
    anywhere = pl.BlockSpec(memory_space=pl.ANY)
    inside = pl.BlockSpec(memory_space=pltpu.VMEM)
    merged, fold, inv, basis = pl.pallas_call(
        sum_kernel,
        out_shape=(
            jax.ShapeDtypeStruct((ROWS, COLS), BF16),
            jax.ShapeDtypeStruct((RANK, COLS), BF16),
            jax.ShapeDtypeStruct((RANK, RANK), F32),
            jax.ShapeDtypeStruct((RANK, ROWS), BF16),
        ),
        in_specs=[anywhere] * 4,
        out_specs=(anywhere, inside, inside, inside),
        scratch_shapes=[
            pltpu.VMEM((TOK, ROWS), BF16),
            pltpu.VMEM((TOK, COLS), BF16),
            pltpu.VMEM((ROWS, COLS), BF16),
            pltpu.VMEM((RANK, COLS), BF16),
            pltpu.VMEM((384, TOK), BF16),
            pltpu.VMEM((ROWS, COLS), BF16),
            pltpu.VMEM((2, RANK, HALF), F32),
            pltpu.VMEM((NX * NY - 1, 8, HALF), F32),
            pltpu.VMEM((8, HALF), F32),
            pltpu.VMEM((8, HALF), F32),
            pltpu.VMEM((8, 384), F32),
            pltpu.VMEM((NZ, 8, 384), F32),
            pltpu.VMEM((8, HALF), F32),
            pltpu.VMEM((8, HALF), F32),
            pltpu.VMEM((RANK, ROWS), F32),
            pltpu.VMEM((RANK, 2 * RANK), F32),
            pltpu.VMEM((RANK, COLS), BF16),
            pltpu.VMEM((2 * NY, 16, HALF), BF16),
            pltpu.VMEM((RANK, COLS), BF16),
            pltpu.VMEM((NZ, 16, HALF), BF16),
            pltpu.SemaphoreType.DMA((14,)),
            pltpu.SemaphoreType.DMA((4,)),
            pltpu.SemaphoreType.DMA((8,)),
            pltpu.SemaphoreType.DMA((8,)),
        ],
        compiler_params=pltpu.CompilerParams(
            collective_id=0, has_side_effects=True, vmem_limit_bytes=56 << 20
        ),
        name="sums",
    )(acts, cotangent, error_prev, q_prev)

    block = 256
    whole = lambda shape: pl.BlockSpec(shape, lambda i: (0, 0))
    error_new, q_new = pl.pallas_call(
        update_kernel,
        grid=(ROWS // block,),
        in_specs=[
            pl.BlockSpec((block, COLS), lambda i: (i, 0)),
            whole((RANK, COLS)),
            whole((RANK, RANK)),
            pl.BlockSpec((RANK, block), lambda i: (0, i)),
        ],
        out_specs=(pl.BlockSpec((block, COLS), lambda i: (i, 0)), whole((RANK, COLS))),
        out_shape=(
            jax.ShapeDtypeStruct((ROWS, COLS), BF16),
            jax.ShapeDtypeStruct((RANK, COLS), F32),
        ),
        scratch_shapes=[pltpu.VMEM((RANK, COLS), BF16)],
        compiler_params=pltpu.CompilerParams(vmem_limit_bytes=40 << 20),
        name="update",
    )(merged, fold, inv, basis)
    return error_new, q_new


def solution(mesh):
    return jax.shard_map(
        body,
        mesh=mesh,
        in_specs=(P("dp", None), P("dp", "tensor"), P("dp", "tensor"), P(None, "tensor")),
        out_specs=(P("dp", "tensor"), P(None, "tensor")),
        check_vma=False,
    )
```

time: 475 us -> 57.8 us (0.12)
  waiting for transfers between devices: 425 us -> 0 us
  Pallas kernels: 0 us -> 52.4 us
  matrix products: 19 us -> 0 us
  between operations: 14.1 us -> 0.65 us
  other arithmetic: 13.1 us -> 0 us
    psum x2 -> x0, waiting for transfers between devices: 425 us -> none  [the longest x1 250 us: body(): project = lax.psum(partial_left, ('dp', 'tensor'))]
    pallas_call x0 -> x2, Pallas kernels: none -> 52.4 us  [the longest x1 48.4 us: body(): pl.pallas_call(sum_kernel, out_shape=(jax.ShapeDtypeStruct((ROWS, COLS),...]
    dot_general x5 -> x0, matrix products: 17.6 us -> none  [the longest x1 6.1 us: body(): lax.dot_general(acts, cotangent, (((0,), (0,)), ((), ())), preferred_elem...]
    another operation x5 -> x0, other arithmetic: 12.1 us -> none  [the longest x3 6.52 us: orthonormal(): lower_factor = jnp.linalg.cholesky(gram_matrix)]
  transfers between devices with their start and end apart: 2 -> 0, of which waited for: 2 -> 0; matrix products, arithmetic and copies ran while one was open for 0% -> 0% of each run, Pallas kernels for 0% -> 0%
where the time goes in v1:
time: 57.8 us; the launch traced here: 57.6 us
  Pallas kernels  52.4 us (91%)
  local copies, waits for them, and re-layouts  4.51 us (8%)
  between operations  0.65 us (1%)
    pallas_call x1, Pallas kernels, body(): pl.pallas_call(sum_kernel, out_shape=(jax.ShapeDtypeStruct((ROWS, COLS),...  48.4 us
    unnamed x8, local copies, waits for them, and re-layouts  4.51 us
    pallas_call x1, Pallas kernels, body(): pl.pallas_call(update_kernel, grid=(ROWS // block,), in_specs=[pl.BlockSp...  3.98 us

profile of v1, /device:TPU:1, one launch (start us, length us, event | category | flops | bytes accessed | tf_op | source)
XLA Modules:
  0.0 57.6 jit_solution(16488339650006397216)
XLA Ops:
  0.6 48.4 %sums.1 = (bf16[1280,1280]{1,0:T(8,128)(2,1)}, bf16[64,1280]{1,0:T(8,128)(2,1)}, f32[64,64]{1,0:T(8,128)}, bf16[64,1280]{1,0:T(8,128)(2,1)}) custom-call(bf16[1024,1280]{1,0:T(8,128)(2,1)} %acts.1, bf16[1024,1280]{1,0:T(8,128)(2,1)} %cot.1, bf16[1280,1280]{1,0:T(8,128)(2,1)} %err.1, bf16[64,1280]{1,0:T(8,128)(2,1)} %q_ref.1), custom_call_target="tpu_custom_call" | custom-call | tf_op jit(solution)/shard_map/sums/pallas_call | solution.py:316
  49.1 0.0 copy-start
  49.1 1.9 %copy-done = bf16[1280,1280]{1,0:T(8,128)(2,1)S(1)} copy-done((bf16[1280,1280]{1,0:T(8,128)(2,1)S(1)}, bf16[1280,1280]{1,0:T(8,128)(2,1)}, u32[]{:S(2)}) %copy-start) | copy-done | bytes 3276824
  51.0 0.0 copy-start.1
  51.0 0.9 %copy-done.1 = bf16[64,1280]{1,0:T(8,128)(2,1)S(1)} copy-done((bf16[64,1280]{1,0:T(8,128)(2,1)S(1)}, bf16[64,1280]{1,0:T(8,128)(2,1)}, u32[]{:S(2)}) %copy-start.1) | copy-done | bytes 163864
  51.9 0.0 copy-start.2
  51.9 0.9 %copy-done.2 = bf16[64,1280]{1,0:T(8,128)(2,1)S(1)} copy-done((bf16[64,1280]{1,0:T(8,128)(2,1)S(1)}, bf16[64,1280]{1,0:T(8,128)(2,1)}, u32[]{:S(2)}) %copy-start.2) | copy-done | bytes 163864
  52.8 0.0 copy-start.3
  52.8 0.8 %copy-done.3 = f32[64,64]{1,0:T(8,128)S(1)} copy-done((f32[64,64]{1,0:T(8,128)S(1)}, f32[64,64]{1,0:T(8,128)}, u32[]{:S(2)}) %copy-start.3) | copy-done | bytes 16408
  53.6 4.0 %update.1 = (bf16[1280,1280]{1,0:T(8,128)(2,1)}, f32[64,1280]{1,0:T(8,128)}) custom-call(bf16[1280,1280]{1,0:T(8,128)(2,1)S(1)} %copy-done, bf16[64,1280]{1,0:T(8,128)(2,1)S(1)} %copy-done.1, f32[64,64]{1,0:T(8,128)S(1)} %copy-done.3, bf16[64,1280]{1,0:T(8,128)(2,1)S(1)} %copy-done.2), custom_call_target="tpu_custom_call" | custom-call | tf_op jit(solution)/shard_map/update/pallas_call | solution.py:360
Async XLA Ops:
  49.1 1.9 %copy-start = (bf16[1280,1280]{1,0:T(8,128)(2,1)S(1)}, bf16[1280,1280]{1,0:T(8,128)(2,1)}, u32[]{:S(2)}) copy-start(bf16[1280,1280]{1,0:T(8,128)(2,1)} %get-tuple-element.6.merged) | copy-start | bytes 9830404
  51.0 0.9 %copy-start.1 = (bf16[64,1280]{1,0:T(8,128)(2,1)S(1)}, bf16[64,1280]{1,0:T(8,128)(2,1)}, u32[]{:S(2)}) copy-start(bf16[64,1280]{1,0:T(8,128)(2,1)} %get-tuple-element.7.fold) | copy-start | bytes 491524
  51.9 0.9 %copy-start.2 = (bf16[64,1280]{1,0:T(8,128)(2,1)S(1)}, bf16[64,1280]{1,0:T(8,128)(2,1)}, u32[]{:S(2)}) copy-start(bf16[64,1280]{1,0:T(8,128)(2,1)} %get-tuple-element.9.basis) | copy-start | bytes 491524
  52.8 0.8 %copy-start.3 = (f32[64,64]{1,0:T(8,128)S(1)}, f32[64,64]{1,0:T(8,128)}, u32[]{:S(2)}) copy-start(f32[64,64]{1,0:T(8,128)} %get-tuple-element.8.inv) | copy-start | bytes 49156

commit v2 on v1

v2 whole, which is shorter than its diff:
```python
import functools

import jax
import jax.numpy as jnp
from jax import lax
from jax.experimental import pallas as pl
from jax.experimental.pallas import tpu as pltpu
from jax.sharding import PartitionSpec as P

ROWS = 1280
COLS = 1280
TOK = 1024
RANK = 64
REPLICAS = 64
NX, NY, NZ = 4, 4, 8
HALF = 640
F32 = jnp.float32
BF16 = jnp.bfloat16
STEP = 256


def device(x, y, z, c):
    return {"dp": (y * NZ + z) * 2 + c, "tensor": x}


def send(src, dst, send_sem, recv_sem, target):
    pltpu.make_async_remote_copy(
        src_ref=src, dst_ref=dst, send_sem=send_sem, recv_sem=recv_sem,
        device_id=target, device_id_type=pl.DeviceIdType.MESH,
    ).start()


def wait_bytes(ref, sem):
    pltpu.make_async_copy(ref, ref, sem).wait()


def hops(d, n):
    return min(d, n - d)


XY = sorted(
    [(dx, dy) for dx in range(NX) for dy in range(NY) if (dx, dy) != (0, 0)],
    key=lambda d: -(hops(d[0], NX) + hops(d[1], NY)),
)
ZS = sorted(range(1, NZ), key=lambda d: -hops(d, NZ))


def slot_xy(dx, dy):
    return dx * NY + dy - 1


def eliminate(first, last, work):
    lane = lax.broadcasted_iota(jnp.int32, (RANK, 2 * RANK), 1)
    row = lax.broadcasted_iota(jnp.int32, (RANK, 2 * RANK), 0)

    def step(k, w):
        pivot_row = jnp.sum(jnp.where(row == k, w, 0.0), axis=0, keepdims=True)
        column = jnp.sum(jnp.where(lane == k, w, 0.0), axis=1, keepdims=True)
        pivot = jnp.sum(
            jnp.where(lane[:1] == k, pivot_row, 0.0), axis=1, keepdims=True
        )
        factor = column / pivot
        return w - jnp.where(row > k, factor * pivot_row, 0.0)

    return lax.fori_loop(first, last, step, work)


def sum_kernel(
    acts, cot, err, q_ref,
    merged, q_new, q_low, basis_out,
    acts_v, cot_v, err_v, q_v, weight, part,
    r1, s1, c1, u1, z1, g1, d1, proj, work,
    fb, fr, fs, z2,
    in_sem, send_sem, recv_sem,
):
    dp = lax.axis_index("dp")
    x = lax.axis_index("tensor")
    c = lax.rem(dp, 2)
    z = lax.rem(dp // 2, NZ)
    y = dp // (2 * NZ)
    other = 1 - c

    def xy_peer(dx, dy):
        return device(lax.rem(x + dx, NX), lax.rem(y + dy, NY), z, c)

    def z_peer(dz):
        return device(x, y, lax.rem(z + dz, NZ), c)

    sibling = device(x, y, z, other)

    copies = [pltpu.make_async_copy(q_ref, q_v, in_sem.at[0])]

    def plan(src, dst, rows, step):
        for r in range(0, rows, step):
            block = pl.ds(r, step)
            copies.append(
                pltpu.make_async_copy(src.at[block], dst.at[block], in_sem.at[len(copies)])
            )

    plan(cot, cot_v, TOK, 512)
    plan(err, err_v, ROWS, STEP)
    plan(acts, acts_v, TOK, STEP)
    turn = [0, 0]

    def start_copies(upto):
        while turn[0] < min(upto, len(copies)):
            copies[turn[0]].start()
            turn[0] += 1

    def next_copy():
        copies[turn[1]].wait()
        turn[1] += 1
        start_copies(turn[1] + 3)

    start_copies(4)
    barrier = pltpu.get_barrier_semaphore()

    def greet(target):
        pl.semaphore_signal(barrier, inc=1, device_id=target, device_id_type=pl.DeviceIdType.MESH)

    for dx, dy in XY:
        greet(xy_peer(dx, dy))
    for dz in ZS:
        greet(z_peer(dz))
    greet(sibling)
    for dy in range(1, NY):
        greet(device(x, lax.rem(y + dy, NY), z, other))

    next_copy()
    for r in range(0, TOK, 512):
        next_copy()
        product = lax.dot_general(
            cot_v[r : r + 512, :], q_v[...], (((1,), (1,)), ((), ())), preferred_element_type=F32
        )
        high = product.astype(BF16)
        low = (product - high.astype(F32)).astype(BF16)
        weight[r : r + 512, :] = jnp.concatenate([high, low], axis=1)
    for r in range(0, ROWS, STEP):
        next_copy()
        part[:, r : r + STEP] = lax.dot_general(
            q_v[...], err_v[r : r + STEP, :], (((1,), (1,)), ((), ())),
            preferred_element_type=F32,
        )
    for r in range(0, TOK, STEP):
        next_copy()
        both = lax.dot_general(
            weight[r : r + STEP, :], acts_v[r : r + STEP, :], (((0,), (0,)), ((), ())),
            preferred_element_type=F32,
        )
        part[...] += both[:RANK] + both[RANK:]
    pl.semaphore_wait(barrier, len(XY) + len(ZS) + NY)
    for dx, dy in XY:
        tx, ty = lax.rem(x + dx, NX), lax.rem(y + dy, NY)
        block = pl.multiple_of((tx * 2 + ty // 2) * 8, 8)
        lanes = pl.ds(pl.multiple_of(lax.rem(ty, 2) * HALF, 128), HALF)
        send(
            part.at[pl.ds(block, 8), lanes], r1.at[slot_xy(dx, dy)],
            send_sem.at[0], recv_sem.at[0], device(tx, ty, z, c),
        )

    for r in range(0, ROWS, STEP):
        grad = lax.dot_general(
            acts_v[:, r : r + STEP], cot_v[...], (((0,), (0,)), ((), ())),
            preferred_element_type=F32,
        )
        merged[r : r + STEP, :] = (grad + err_v[r : r + STEP, :].astype(F32)).astype(BF16)

    mine = pl.multiple_of((x * 2 + y // 2) * 8, 8)
    wait_bytes(r1, recv_sem.at[0])
    lanes = pl.ds(pl.multiple_of(lax.rem(y, 2) * HALF, 128), HALF)
    total = part[pl.ds(mine, 8), lanes]
    for i in range(NX * NY - 1):
        total = total + r1[i]
    s1[...] = total
    send(s1, c1, send_sem.at[1], recv_sem.at[1], sibling)
    wait_bytes(c1, recv_sem.at[1])
    g1[...] = s1[...] + c1[...]
    own = pl.multiple_of(c * 256, 128)
    u1[...] = g1[:, pl.ds(own, 384)]
    for dz in ZS:
        send(u1, z1.at[z], send_sem.at[2], recv_sem.at[2], z_peer(dz))
    z1[z] = u1[...]
    wait_bytes(z1.at[pl.ds(0, NZ - 1)], recv_sem.at[2])
    total = z1[0]
    for i in range(1, NZ):
        total = total + z1[i]
    d1[:, pl.ds(own, 384)] = total
    give = pl.multiple_of(c * 384, 128)
    send(
        d1.at[:, pl.ds(give, 256)], d1.at[:, pl.ds(give, 256)],
        send_sem.at[3], recv_sem.at[3], sibling,
    )
    wait_bytes(d1.at[:, pl.ds(0, 256)], recv_sem.at[3])
    home = proj.at[pl.ds(mine, 8), lanes]
    for dx, dy in XY:
        send(d1, home, send_sem.at[4], recv_sem.at[4], xy_peer(dx, dy))
    proj[pl.ds(mine, 8), lanes] = d1[...]
    wait_bytes(r1, recv_sem.at[4])

    left = proj[...]
    high = left.astype(BF16)
    low = (left - high.astype(F32)).astype(BF16)
    stack = jnp.concatenate([high, low], axis=0)
    for h in range(2):
        both = jnp.dot(stack, merged[:, h * HALF : (h + 1) * HALF], preferred_element_type=F32)
        fb[:, h * HALF : (h + 1) * HALF] = (both[:RANK] + both[RANK:]).astype(BF16)
        for dy in (2, 1, 3, 0):
            ty = lax.rem(y + dy, NY)
            rows = pl.ds(pl.multiple_of(ty * 16, 16), 16)

            def give_fold():
                send(
                    fb.at[rows, pl.ds(h * HALF, HALF)], fr.at[y * 2 + c],
                    send_sem.at[5], recv_sem.at[5], device(x, ty, z, h),
                )

            if dy:
                give_fold()
            else:
                pl.when(c != h)(give_fold)
    fr[y * 2 + c] = fb[
        pl.ds(pl.multiple_of(y * 16, 16), 16), pl.ds(pl.multiple_of(c * HALF, 128), HALF)
    ]

    gram = lax.dot_general(
        left, left, (((1,), (1,)), ((), ())),
        precision=lax.Precision.HIGHEST, preferred_element_type=F32,
    )
    eye = (
        lax.broadcasted_iota(jnp.int32, (RANK, RANK), 0)
        == lax.broadcasted_iota(jnp.int32, (RANK, RANK), 1)
    ).astype(F32)
    work[...] = eliminate(0, 20, jnp.concatenate([gram, eye], axis=1))

    wait_bytes(fr.at[pl.ds(0, 2 * NY - 1)], recv_sem.at[5])
    total = fr[0].astype(F32)
    for i in range(1, 2 * NY):
        total = total + fr[i].astype(F32)
    z2[z] = total.astype(BF16)
    for dz in ZS:
        send(z2.at[z], z2.at[z], send_sem.at[6], recv_sem.at[6], z_peer(dz))
    work[...] = eliminate(20, RANK, work[...])
    wait_bytes(z2.at[pl.ds(0, NZ - 1)], recv_sem.at[6])
    total = z2[0].astype(F32)
    for i in range(1, NZ):
        total = total + z2[i].astype(F32)
    rows = pl.ds(pl.multiple_of(y * 16, 16), 16)
    lanes = pl.ds(pl.multiple_of(c * HALF, 128), HALF)
    fs[rows, lanes] = total.astype(BF16)
    for dy in (2, 1, 3):
        ty = lax.rem(y + dy, NY)
        for core in (other, c):
            send(
                fs.at[rows, lanes], fs.at[rows, lanes],
                send_sem.at[7], recv_sem.at[7], device(x, ty, z, core),
            )
    send(fs.at[rows, lanes], fs.at[rows, lanes], send_sem.at[7], recv_sem.at[7], sibling)

    eliminated = work[...]
    diagonal = jnp.sum(eliminated[:, :RANK] * eye, axis=1, keepdims=True)
    inverse = eliminated[:, RANK:] * lax.rsqrt(diagonal)
    basis_out[...] = jnp.dot(
        inverse, proj[...], precision=lax.Precision.HIGHEST, preferred_element_type=F32
    ).astype(BF16)

    wait_bytes(fr.at[pl.ds(0, 2 * NY - 1)], recv_sem.at[7])
    q = jnp.dot(
        inverse, fs[...].astype(F32), precision=lax.Precision.HIGHEST, preferred_element_type=F32
    ) * (1.0 / REPLICAS)
    q_new[...] = q
    q_low[...] = q.astype(BF16)


    wait_bytes(r1, send_sem.at[0])
    wait_bytes(s1, send_sem.at[1])
    wait_bytes(z1.at[pl.ds(0, NZ - 1)], send_sem.at[2])
    wait_bytes(d1.at[:, pl.ds(0, 256)], send_sem.at[3])
    wait_bytes(r1, send_sem.at[4])
    wait_bytes(fr.at[pl.ds(0, 2 * NY - 1)], send_sem.at[5])
    wait_bytes(z2.at[pl.ds(0, NZ - 1)], send_sem.at[6])
    wait_bytes(fr.at[pl.ds(0, 2 * NY - 1)], send_sem.at[7])


def update_kernel(merged, q_in, q_low, basis, error_new, q_new, error_v, sem):
    copies = [pltpu.make_async_copy(q_in, q_new, sem.at[0])]
    copies[0].start()
    for r in range(0, ROWS, STEP):
        low_rank = lax.dot_general(
            basis[:, r : r + STEP], q_low[...], (((0,), (0,)), ((), ())),
            preferred_element_type=F32,
        )
        error_v[r : r + STEP, :] = (merged[r : r + STEP, :].astype(F32) - low_rank).astype(BF16)
        block = pl.ds(r, STEP)
        copies.append(
            pltpu.make_async_copy(error_v.at[block], error_new.at[block], sem.at[len(copies)])
        )
        copies[-1].start()
    for copy in copies:
        copy.wait()


def body(acts, cotangent, error_prev, q_prev):
    anywhere = pl.BlockSpec(memory_space=pl.ANY)
    inside = pl.BlockSpec(memory_space=pltpu.VMEM)
    outside = [
        pltpu.with_memory_space_constraint(a, pltpu.HBM)
        for a in (acts, cotangent, error_prev, q_prev)
    ]
    results = pl.pallas_call(
        sum_kernel,
        out_shape=(
            pltpu.VMEM((ROWS, COLS), BF16),
            pltpu.VMEM((RANK, COLS), F32),
            pltpu.VMEM((RANK, COLS), BF16),
            pltpu.VMEM((RANK, ROWS), BF16),
        ),
        in_specs=[anywhere] * 4,
        out_specs=(inside,) * 4,
        scratch_shapes=[
            pltpu.VMEM((TOK, ROWS), BF16),
            pltpu.VMEM((TOK, COLS), BF16),
            pltpu.VMEM((ROWS, COLS), BF16),
            pltpu.VMEM((RANK, COLS), BF16),
            pltpu.VMEM((TOK, 2 * RANK), BF16),
            pltpu.VMEM((RANK, ROWS), F32),
            pltpu.VMEM((NX * NY - 1, 8, HALF), F32),
            pltpu.VMEM((8, HALF), F32),
            pltpu.VMEM((8, HALF), F32),
            pltpu.VMEM((8, 384), F32),
            pltpu.VMEM((NZ, 8, 384), F32),
            pltpu.VMEM((8, HALF), F32),
            pltpu.VMEM((8, HALF), F32),
            pltpu.VMEM((RANK, ROWS), F32),
            pltpu.VMEM((RANK, 2 * RANK), F32),
            pltpu.VMEM((RANK, COLS), BF16),
            pltpu.VMEM((2 * NY, 16, HALF), BF16),
            pltpu.VMEM((RANK, COLS), BF16),
            pltpu.VMEM((NZ, 16, HALF), BF16),
            pltpu.SemaphoreType.DMA((12,)),
            pltpu.SemaphoreType.DMA((8,)),
            pltpu.SemaphoreType.DMA((8,)),
        ],
        compiler_params=pltpu.CompilerParams(
            collective_id=0, has_side_effects=True, vmem_limit_bytes=40 << 20
        ),
        name="sums",
    )(*outside)
    results = [pltpu.with_memory_space_constraint(a, pltpu.VMEM) for a in results]
    return pl.pallas_call(
        update_kernel,
        in_specs=[inside] * 4,
        out_specs=(anywhere, anywhere),
        out_shape=(
            jax.ShapeDtypeStruct((ROWS, COLS), BF16),
            jax.ShapeDtypeStruct((RANK, COLS), F32),
        ),
        scratch_shapes=[
            pltpu.VMEM((ROWS, COLS), BF16),
            pltpu.SemaphoreType.DMA((1 + ROWS // STEP,)),
        ],
        compiler_params=pltpu.CompilerParams(vmem_limit_bytes=40 << 20),
        name="update",
    )(*results)


def solution(mesh):
    return jax.shard_map(
        body,
        mesh=mesh,
        in_specs=(P("dp", None), P("dp", "tensor"), P("dp", "tensor"), P(None, "tensor")),
        out_specs=(P("dp", "tensor"), P(None, "tensor")),
        check_vma=False,
    )
```

time: 57.8 us -> 50.4 us (0.87)
  local copies, waits for them, and re-layouts: 4.51 us -> 0 us
  Pallas kernels: 52.4 us -> 49.6 us
    unnamed x8 -> x0, local copies, waits for them, and re-layouts: 4.51 us -> none
    pallas_call x2, Pallas kernels: 52.4 us -> 49.6 us  [the longest x1 47.5 us: body(): pl.pallas_call(sum_kernel, out_shape=(pltpu.VMEM((ROWS, COLS), BF16), plt...]
where the time goes in v2:
time: 50.4 us; the launch traced here: 50.3 us
  Pallas kernels  49.6 us (98%)
  between operations  0.64 us (1%)
    pallas_call x1, Pallas kernels, body(): pl.pallas_call(sum_kernel, out_shape=(pltpu.VMEM((ROWS, COLS), BF16), plt...  47.5 us
    pallas_call x1, Pallas kernels, body(): pl.pallas_call(update_kernel, in_specs=[inside] * 4, out_specs=(anywhere,...  2.11 us

profile of v2, /device:TPU:1, one launch (start us, length us, event | category | flops | bytes accessed | tf_op | source)
XLA Modules:
  0.0 50.3 jit_solution(13541902503345661669)
XLA Ops:
  0.6 47.5 %sums.1 = (bf16[1280,1280]{1,0:T(8,128)(2,1)S(1)}, f32[64,1280]{1,0:T(8,128)S(1)}, bf16[64,1280]{1,0:T(8,128)(2,1)S(1)}, bf16[64,1280]{1,0:T(8,128)(2,1)S(1)}) custom-call(bf16[1024,1280]{1,0:T(8,128)(2,1)} %acts.1, bf16[1024,1280]{1,0:T(8,128)(2,1)} %cot.1, bf16[1280,1280]{1,0:T(8,128)(2,1)} %err.1, bf16[64,1280]{1,0:T(8,128)(2,1)} %q_ref.1), custom_call_target="tpu_custom_call" | custom-call | tf_op jit(solution)/shard_map/sums/pallas_call | solution.py:309
  48.2 2.1 %update.1 = (bf16[1280,1280]{1,0:T(8,128)(2,1)}, f32[64,1280]{1,0:T(8,128)}) custom-call(bf16[1280,1280]{1,0:T(8,128)(2,1)S(1)} %get-tuple-element.6.merged, f32[64,1280]{1,0:T(8,128)S(1)} %get-tuple-element.7.q_in, bf16[64,1280]{1,0:T(8,128)(2,1)S(1)} %get-tuple-element.8.q_low, bf16[64,1280]{1,0:T(8,128)(2,1)S(1)} %get-tuple-element.9.basis), custom_call_target="tpu_custom_call" | custom-call | tf_op jit(solution)/shard_map/update/pallas_call | solution.py:349

commit v3 on v2

--- a/solution.py
+++ b/solution.py
@@ -14,6 +14,7 @@
 REPLICAS = 64
 NX, NY, NZ = 4, 4, 8
 HALF = 640
+WIDE = 384
 F32 = jnp.float32
 BF16 = jnp.bfloat16
 STEP = 256
@@ -45,6 +46,22 @@
 ZS = sorted(range(1, NZ), key=lambda d: -hops(d, NZ))
 
 
+def ranks(i):
+    return pl.ds(pl.multiple_of(i * 8, 8), 8)
+
+
+def lanes(j):
+    return pl.ds(pl.multiple_of(j * 256 + j // 2 * 128, 128), WIDE)
+
+
+def sixteen(i):
+    return pl.ds(pl.multiple_of(i * 16, 16), 16)
+
+
+def lane_half(i):
+    return pl.ds(pl.multiple_of(i * HALF, 128), HALF)
+
+
 def slot_xy(dx, dy):
     return dx * NY + dy - 1
 
@@ -69,9 +86,9 @@
     acts, cot, err, q_ref,
     merged, q_new, q_low, basis_out,
     acts_v, cot_v, err_v, q_v, weight, part,
-    r1, s1, c1, u1, z1, g1, d1, proj, work,
+    c0, half, twin, r1, z1, g1, proj, work,
     fb, fr, fs, z2,
-    in_sem, send_sem, recv_sem,
+    in_sem, core_send, core_recv, send_sem, recv_sem,
 ):
     dp = lax.axis_index("dp")
     x = lax.axis_index("tensor")
@@ -90,16 +107,12 @@
 
     copies = [pltpu.make_async_copy(q_ref, q_v, in_sem.at[0])]
 
-    def plan(src, dst, rows, step):
-        for r in range(0, rows, step):
-            block = pl.ds(r, step)
-            copies.append(
-                pltpu.make_async_copy(src.at[block], dst.at[block], in_sem.at[len(copies)])
-            )
-
-    plan(cot, cot_v, TOK, 512)
-    plan(err, err_v, ROWS, STEP)
-    plan(acts, acts_v, TOK, STEP)
+    def plan(pairs):
+        for src, dst in pairs:
+            copies.append(pltpu.make_async_copy(src, dst, in_sem.at[len(copies)]))
+
+    plan([(cot.at[pl.ds(r, 512)], cot_v.at[pl.ds(r, 512)]) for r in range(0, TOK, 512)])
+    plan([(err, err_v), (acts, acts_v)])
     turn = [0, 0]
 
     def start_copies(upto):
@@ -135,26 +148,35 @@
         high = product.astype(BF16)
         low = (product - high.astype(F32)).astype(BF16)
         weight[r : r + 512, :] = jnp.concatenate([high, low], axis=1)
+    next_copy()
     for r in range(0, ROWS, STEP):
-        next_copy()
         part[:, r : r + STEP] = lax.dot_general(
             q_v[...], err_v[r : r + STEP, :], (((1,), (1,)), ((), ())),
             preferred_element_type=F32,
         )
-    for r in range(0, TOK, STEP):
-        next_copy()
+    ours = pl.ds(pl.multiple_of(c * 32, 32), 32)
+    theirs = pl.ds(pl.multiple_of(other * 32, 32), 32)
+    next_copy()
+    for i, r in enumerate(range(0, ROWS, STEP)):
         both = lax.dot_general(
-            weight[r : r + STEP, :], acts_v[r : r + STEP, :], (((0,), (0,)), ((), ())),
+            weight[...], acts_v[:, r : r + STEP], (((0,), (0,)), ((), ())),
             preferred_element_type=F32,
         )
-        part[...] += both[:RANK] + both[RANK:]
-    pl.semaphore_wait(barrier, len(XY) + len(ZS) + NY)
+        part[:, r : r + STEP] += both[:RANK] + both[RANK:]
+        if i == 0:
+            pl.semaphore_wait(barrier, len(XY) + len(ZS) + NY)
+        columns = pl.ds(r, STEP)
+        send(
+            part.at[theirs, columns], c0.at[:, columns], core_send.at[i], core_recv.at[i], sibling
+        )
+    for i, r in enumerate(range(0, ROWS, STEP)):
+        columns = pl.ds(r, STEP)
+        wait_bytes(c0.at[:, columns], core_recv.at[i])
+        half[:, columns] = part[ours, columns] + c0[:, columns]
     for dx, dy in XY:
         tx, ty = lax.rem(x + dx, NX), lax.rem(y + dy, NY)
-        block = pl.multiple_of((tx * 2 + ty // 2) * 8, 8)
-        lanes = pl.ds(pl.multiple_of(lax.rem(ty, 2) * HALF, 128), HALF)
         send(
-            part.at[pl.ds(block, 8), lanes], r1.at[slot_xy(dx, dy)],
+            half.at[ranks(tx), lanes(ty)], r1.at[slot_xy(dx, dy)],
             send_sem.at[0], recv_sem.at[0], device(tx, ty, z, c),
         )
 
@@ -164,64 +186,55 @@
             preferred_element_type=F32,
         )
         merged[r : r + STEP, :] = (grad + err_v[r : r + STEP, :].astype(F32)).astype(BF16)
-
-    mine = pl.multiple_of((x * 2 + y // 2) * 8, 8)
+        block = pl.ds(r, STEP)
+        send(merged.at[block], twin.at[block], send_sem.at[4], recv_sem.at[4], sibling)
+
     wait_bytes(r1, recv_sem.at[0])
-    lanes = pl.ds(pl.multiple_of(lax.rem(y, 2) * HALF, 128), HALF)
-    total = part[pl.ds(mine, 8), lanes]
+    total = half[ranks(x), lanes(y)]
     for i in range(NX * NY - 1):
         total = total + r1[i]
-    s1[...] = total
-    send(s1, c1, send_sem.at[1], recv_sem.at[1], sibling)
-    wait_bytes(c1, recv_sem.at[1])
-    g1[...] = s1[...] + c1[...]
-    own = pl.multiple_of(c * 256, 128)
-    u1[...] = g1[:, pl.ds(own, 384)]
+    z1[z] = total
     for dz in ZS:
-        send(u1, z1.at[z], send_sem.at[2], recv_sem.at[2], z_peer(dz))
-    z1[z] = u1[...]
-    wait_bytes(z1.at[pl.ds(0, NZ - 1)], recv_sem.at[2])
+        send(z1.at[z], z1.at[z], send_sem.at[1], recv_sem.at[1], z_peer(dz))
+    wait_bytes(z1.at[pl.ds(0, NZ - 1)], recv_sem.at[1])
     total = z1[0]
     for i in range(1, NZ):
         total = total + z1[i]
-    d1[:, pl.ds(own, 384)] = total
-    give = pl.multiple_of(c * 384, 128)
-    send(
-        d1.at[:, pl.ds(give, 256)], d1.at[:, pl.ds(give, 256)],
-        send_sem.at[3], recv_sem.at[3], sibling,
-    )
-    wait_bytes(d1.at[:, pl.ds(0, 256)], recv_sem.at[3])
-    home = proj.at[pl.ds(mine, 8), lanes]
+    mine = x * NY + y
+    g1[mine] = total
     for dx, dy in XY:
-        send(d1, home, send_sem.at[4], recv_sem.at[4], xy_peer(dx, dy))
-    proj[pl.ds(mine, 8), lanes] = d1[...]
-    wait_bytes(r1, recv_sem.at[4])
-
-    left = proj[...]
+        send(g1.at[mine], g1.at[mine], send_sem.at[2], recv_sem.at[2], xy_peer(dx, dy))
+    wait_bytes(r1, recv_sem.at[2])
+    for i in range(NX):
+        for j in range(NY):
+            start = j * 256 + j // 2 * 128
+            c0[8 * i : 8 * i + 8, start : start + WIDE] = g1[i * NY + j]
+    send(c0, proj.at[ours], send_sem.at[3], recv_sem.at[3], sibling)
+    wait_bytes(twin, recv_sem.at[4])
+    left = c0[...]
     high = left.astype(BF16)
     low = (left - high.astype(F32)).astype(BF16)
     stack = jnp.concatenate([high, low], axis=0)
     for h in range(2):
-        both = jnp.dot(stack, merged[:, h * HALF : (h + 1) * HALF], preferred_element_type=F32)
-        fb[:, h * HALF : (h + 1) * HALF] = (both[:RANK] + both[RANK:]).astype(BF16)
-        for dy in (2, 1, 3, 0):
+        columns = pl.ds(h * HALF, HALF)
+        both = jnp.dot(stack, merged[:, columns], preferred_element_type=F32)
+        both = both + jnp.dot(stack, twin[:, columns], preferred_element_type=F32)
+        fb[:, columns] = (both[:32] + both[32:]).astype(BF16)
+        for dy in (2, 1, 3):
             ty = lax.rem(y + dy, NY)
-            rows = pl.ds(pl.multiple_of(ty * 16, 16), 16)
-
-            def give_fold():
+
+            @pl.when(lax.rem(ty, 2) == h)
+            def _():
                 send(
-                    fb.at[rows, pl.ds(h * HALF, HALF)], fr.at[y * 2 + c],
-                    send_sem.at[5], recv_sem.at[5], device(x, ty, z, h),
+                    fb.at[sixteen(ty // 2), columns], fr.at[y],
+                    send_sem.at[5], recv_sem.at[5], device(x, ty, z, c),
                 )
 
-            if dy:
-                give_fold()
-            else:
-                pl.when(c != h)(give_fold)
-    fr[y * 2 + c] = fb[
-        pl.ds(pl.multiple_of(y * 16, 16), 16), pl.ds(pl.multiple_of(c * HALF, 128), HALF)
-    ]
-
+    fr[y] = fb[sixteen(y // 2), lane_half(lax.rem(y, 2))]
+
+    proj[ours, :] = left
+    wait_bytes(half, recv_sem.at[3])
+    left = proj[...]
     gram = lax.dot_general(
         left, left, (((1,), (1,)), ((), ())),
         precision=lax.Precision.HIGHEST, preferred_element_type=F32,
@@ -230,55 +243,60 @@
         lax.broadcasted_iota(jnp.int32, (RANK, RANK), 0)
         == lax.broadcasted_iota(jnp.int32, (RANK, RANK), 1)
     ).astype(F32)
-    work[...] = eliminate(0, 20, jnp.concatenate([gram, eye], axis=1))
-
-    wait_bytes(fr.at[pl.ds(0, 2 * NY - 1)], recv_sem.at[5])
+    work[...] = eliminate(0, 12, jnp.concatenate([gram, eye], axis=1))
+
+    wait_bytes(fr.at[pl.ds(0, NY - 1)], recv_sem.at[5])
     total = fr[0].astype(F32)
-    for i in range(1, 2 * NY):
+    for i in range(1, NY):
         total = total + fr[i].astype(F32)
     z2[z] = total.astype(BF16)
     for dz in ZS:
         send(z2.at[z], z2.at[z], send_sem.at[6], recv_sem.at[6], z_peer(dz))
-    work[...] = eliminate(20, RANK, work[...])
+    work[...] = eliminate(12, 46, work[...])
     wait_bytes(z2.at[pl.ds(0, NZ - 1)], recv_sem.at[6])
     total = z2[0].astype(F32)
     for i in range(1, NZ):
         total = total + z2[i].astype(F32)
-    rows = pl.ds(pl.multiple_of(y * 16, 16), 16)
-    lanes = pl.ds(pl.multiple_of(c * HALF, 128), HALF)
-    fs[rows, lanes] = total.astype(BF16)
+    here = fs.at[sixteen(2 * c + y // 2), lane_half(lax.rem(y, 2))]
+    landed = z2.at[pl.ds(0, NZ - 1)]
+    here[...] = total.astype(BF16)
     for dy in (2, 1, 3):
         ty = lax.rem(y + dy, NY)
         for core in (other, c):
             send(
-                fs.at[rows, lanes], fs.at[rows, lanes],
+                here, here,
                 send_sem.at[7], recv_sem.at[7], device(x, ty, z, core),
             )
-    send(fs.at[rows, lanes], fs.at[rows, lanes], send_sem.at[7], recv_sem.at[7], sibling)
-
-    eliminated = work[...]
+    send(here, here, send_sem.at[7], recv_sem.at[7], sibling)
+
+    eliminated = eliminate(46, RANK, work[...])
     diagonal = jnp.sum(eliminated[:, :RANK] * eye, axis=1, keepdims=True)
     inverse = eliminated[:, RANK:] * lax.rsqrt(diagonal)
     basis_out[...] = jnp.dot(
         inverse, proj[...], precision=lax.Precision.HIGHEST, preferred_element_type=F32
     ).astype(BF16)
 
-    wait_bytes(fr.at[pl.ds(0, 2 * NY - 1)], recv_sem.at[7])
-    q = jnp.dot(
-        inverse, fs[...].astype(F32), precision=lax.Precision.HIGHEST, preferred_element_type=F32
-    ) * (1.0 / REPLICAS)
+    wait_bytes(landed, recv_sem.at[7])
+    high = inverse.astype(BF16)
+    low = (inverse - high.astype(F32)).astype(BF16)
+    both = jnp.dot(
+        jnp.concatenate([high, low], axis=0), fs[...], preferred_element_type=F32
+    )
+    q = (both[:RANK] + both[RANK:]) * (1.0 / REPLICAS)
     q_new[...] = q
     q_low[...] = q.astype(BF16)
 
 
+    for i, r in enumerate(range(0, ROWS, STEP)):
+        wait_bytes(c0.at[:, pl.ds(r, STEP)], core_send.at[i])
     wait_bytes(r1, send_sem.at[0])
-    wait_bytes(s1, send_sem.at[1])
-    wait_bytes(z1.at[pl.ds(0, NZ - 1)], send_sem.at[2])
-    wait_bytes(d1.at[:, pl.ds(0, 256)], send_sem.at[3])
-    wait_bytes(r1, send_sem.at[4])
-    wait_bytes(fr.at[pl.ds(0, 2 * NY - 1)], send_sem.at[5])
+    wait_bytes(z1.at[pl.ds(0, NZ - 1)], send_sem.at[1])
+    wait_bytes(r1, send_sem.at[2])
+    wait_bytes(half, send_sem.at[3])
+    wait_bytes(twin, send_sem.at[4])
+    wait_bytes(fr.at[pl.ds(0, NY - 1)], send_sem.at[5])
     wait_bytes(z2.at[pl.ds(0, NZ - 1)], send_sem.at[6])
-    wait_bytes(fr.at[pl.ds(0, 2 * NY - 1)], send_sem.at[7])
+    wait_bytes(landed, send_sem.at[7])
 
 
 def update_kernel(merged, q_in, q_low, basis, error_new, q_new, error_v, sem):
@@ -323,20 +341,21 @@
             pltpu.VMEM((RANK, COLS), BF16),
             pltpu.VMEM((TOK, 2 * RANK), BF16),
             pltpu.VMEM((RANK, ROWS), F32),
-            pltpu.VMEM((NX * NY - 1, 8, HALF), F32),
-            pltpu.VMEM((8, HALF), F32),
-            pltpu.VMEM((8, HALF), F32),
-            pltpu.VMEM((8, 384), F32),
-            pltpu.VMEM((NZ, 8, 384), F32),
-            pltpu.VMEM((8, HALF), F32),
-            pltpu.VMEM((8, HALF), F32),
+            pltpu.VMEM((RANK // 2, ROWS), F32),
+            pltpu.VMEM((RANK // 2, ROWS), F32),
+            pltpu.VMEM((ROWS, COLS), BF16),
+            pltpu.VMEM((NX * NY - 1, 8, WIDE), F32),
+            pltpu.VMEM((NZ, 8, WIDE), F32),
+            pltpu.VMEM((NX * NY, 8, WIDE), F32),
             pltpu.VMEM((RANK, ROWS), F32),
             pltpu.VMEM((RANK, 2 * RANK), F32),
-            pltpu.VMEM((RANK, COLS), BF16),
-            pltpu.VMEM((2 * NY, 16, HALF), BF16),
+            pltpu.VMEM((RANK // 2, COLS), BF16),
+            pltpu.VMEM((NY, 16, HALF), BF16),
             pltpu.VMEM((RANK, COLS), BF16),
             pltpu.VMEM((NZ, 16, HALF), BF16),
-            pltpu.SemaphoreType.DMA((12,)),
+            pltpu.SemaphoreType.DMA((5,)),
+            pltpu.SemaphoreType.DMA((5,)),
+            pltpu.SemaphoreType.DMA((5,)),
             pltpu.SemaphoreType.DMA((8,)),
             pltpu.SemaphoreType.DMA((8,)),
         ],

time: 50.4 us -> 46.5 us (0.923)
  Pallas kernels: 49.6 us -> 45.8 us
    pallas_call x1, Pallas kernels: 47.5 us -> 43.7 us  [body(): pl.pallas_call(sum_kernel, out_shape=(pltpu.VMEM((ROWS, COLS), BF16), plt...]
where the time goes in v3:
time: 46.5 us; the launch traced here: 46.4 us
  Pallas kernels  45.8 us (98%)
  between operations  0.64 us (1%)
    pallas_call x1, Pallas kernels, body(): pl.pallas_call(sum_kernel, out_shape=(pltpu.VMEM((ROWS, COLS), BF16), plt...  43.7 us
    pallas_call x1, Pallas kernels, body(): pl.pallas_call(update_kernel, in_specs=[inside] * 4, out_specs=(anywhere,...  2.11 us

profile of v3, /device:TPU:1, one launch (start us, length us, event | category | flops | bytes accessed | tf_op | source)
XLA Modules:
  0.0 46.4 jit_solution(18422437744663471861)
XLA Ops:
  0.6 43.7 %sums.1 = (bf16[1280,1280]{1,0:T(8,128)(2,1)S(1)}, f32[64,1280]{1,0:T(8,128)S(1)}, bf16[64,1280]{1,0:T(8,128)(2,1)S(1)}, bf16[64,1280]{1,0:T(8,128)(2,1)S(1)}) custom-call(bf16[1024,1280]{1,0:T(8,128)(2,1)} %acts.1, bf16[1024,1280]{1,0:T(8,128)(2,1)} %cot.1, bf16[1280,1280]{1,0:T(8,128)(2,1)} %err.1, bf16[64,1280]{1,0:T(8,128)(2,1)} %q_ref.1), custom_call_target="tpu_custom_call" | custom-call | tf_op jit(solution)/shard_map/sums/pallas_call | solution.py:327
  44.3 2.1 %update.1 = (bf16[1280,1280]{1,0:T(8,128)(2,1)}, f32[64,1280]{1,0:T(8,128)}) custom-call(bf16[1280,1280]{1,0:T(8,128)(2,1)S(1)} %get-tuple-element.6.merged, f32[64,1280]{1,0:T(8,128)S(1)} %get-tuple-element.7.q_in, bf16[64,1280]{1,0:T(8,128)(2,1)S(1)} %get-tuple-element.8.q_low, bf16[64,1280]{1,0:T(8,128)(2,1)S(1)} %get-tuple-element.9.basis), custom_call_target="tpu_custom_call" | custom-call | tf_op jit(solution)/shard_map/update/pallas_call | solution.py:368

commit v4 on v3

--- a/solution.py
+++ b/solution.py
@@ -14,10 +14,11 @@
 REPLICAS = 64
 NX, NY, NZ = 4, 4, 8
 HALF = 640
-WIDE = 384
 F32 = jnp.float32
 BF16 = jnp.bfloat16
 STEP = 256
+GROUPS = ROWS // STEP
+OWNERS = 2 * GROUPS
 
 
 def device(x, y, z, c):
@@ -46,24 +47,12 @@
 ZS = sorted(range(1, NZ), key=lambda d: -hops(d, NZ))
 
 
-def ranks(i):
-    return pl.ds(pl.multiple_of(i * 8, 8), 8)
-
-
-def lanes(j):
-    return pl.ds(pl.multiple_of(j * 256 + j // 2 * 128, 128), WIDE)
-
-
 def sixteen(i):
     return pl.ds(pl.multiple_of(i * 16, 16), 16)
 
 
 def lane_half(i):
     return pl.ds(pl.multiple_of(i * HALF, 128), HALF)
-
-
-def slot_xy(dx, dy):
-    return dx * NY + dy - 1
 
 
 def eliminate(first, last, work):
@@ -86,7 +75,7 @@
     acts, cot, err, q_ref,
     merged, q_new, q_low, basis_out,
     acts_v, cot_v, err_v, q_v, weight, part,
-    c0, half, twin, r1, z1, g1, proj, work,
+    c0, half, twin, r1, z1, g1, left, proj, work,
     fb, fr, fs, z2,
     in_sem, core_send, core_recv, send_sem, recv_sem,
 ):
@@ -112,7 +101,8 @@
             copies.append(pltpu.make_async_copy(src, dst, in_sem.at[len(copies)]))
 
     plan([(cot.at[pl.ds(r, 512)], cot_v.at[pl.ds(r, 512)]) for r in range(0, TOK, 512)])
-    plan([(err, err_v), (acts, acts_v)])
+    plan([(err, err_v)])
+    plan([(acts.at[pl.ds(r, 512)], acts_v.at[pl.ds(r, 512)]) for r in range(0, TOK, 512)])
     turn = [0, 0]
 
     def start_copies(upto):
@@ -157,9 +147,14 @@
     ours = pl.ds(pl.multiple_of(c * 32, 32), 32)
     theirs = pl.ds(pl.multiple_of(other * 32, 32), 32)
     next_copy()
+    both = lax.dot_general(
+        weight[:512, :], acts_v[:512, :], (((0,), (0,)), ((), ())), preferred_element_type=F32
+    )
+    part[...] += both[:RANK] + both[RANK:]
+    next_copy()
     for i, r in enumerate(range(0, ROWS, STEP)):
         both = lax.dot_general(
-            weight[...], acts_v[:, r : r + STEP], (((0,), (0,)), ((), ())),
+            weight[512:, :], acts_v[512:, r : r + STEP], (((0,), (0,)), ((), ())),
             preferred_element_type=F32,
         )
         part[:, r : r + STEP] += both[:RANK] + both[RANK:]
@@ -169,16 +164,19 @@
         send(
             part.at[theirs, columns], c0.at[:, columns], core_send.at[i], core_recv.at[i], sibling
         )
-    for i, r in enumerate(range(0, ROWS, STEP)):
-        columns = pl.ds(r, STEP)
+    mine = x * NY + y
+    for i in range(GROUPS):
+        columns = pl.ds(i * STEP, STEP)
         wait_bytes(c0.at[:, columns], core_recv.at[i])
-        half[:, columns] = part[ours, columns] + c0[:, columns]
-    for dx, dy in XY:
-        tx, ty = lax.rem(x + dx, NX), lax.rem(y + dy, NY)
-        send(
-            half.at[ranks(tx), lanes(ty)], r1.at[slot_xy(dx, dy)],
-            send_sem.at[0], recv_sem.at[0], device(tx, ty, z, c),
-        )
+        half[:, columns] = (part[ours, columns] + c0[:, columns]).astype(BF16)
+        for owner in (i, GROUPS + i):
+
+            @pl.when(mine != owner)
+            def _():
+                send(
+                    half.at[pl.ds(owner // GROUPS * 16, 16), columns], r1.at[mine],
+                    send_sem.at[0], recv_sem.at[0], device(owner // NY, owner % NY, z, c),
+                )
 
     for r in range(0, ROWS, STEP):
         grad = lax.dot_general(
@@ -189,37 +187,41 @@
         block = pl.ds(r, STEP)
         send(merged.at[block], twin.at[block], send_sem.at[4], recv_sem.at[4], sibling)
 
-    wait_bytes(r1, recv_sem.at[0])
-    total = half[ranks(x), lanes(y)]
-    for i in range(NX * NY - 1):
-        total = total + r1[i]
-    z1[z] = total
-    for dz in ZS:
-        send(z1.at[z], z1.at[z], send_sem.at[1], recv_sem.at[1], z_peer(dz))
-    wait_bytes(z1.at[pl.ds(0, NZ - 1)], recv_sem.at[1])
-    total = z1[0]
-    for i in range(1, NZ):
-        total = total + z1[i]
-    mine = x * NY + y
-    g1[mine] = total
-    for dx, dy in XY:
-        send(g1.at[mine], g1.at[mine], send_sem.at[2], recv_sem.at[2], xy_peer(dx, dy))
-    wait_bytes(r1, recv_sem.at[2])
-    for i in range(NX):
-        for j in range(NY):
-            start = j * 256 + j // 2 * 128
-            c0[8 * i : 8 * i + 8, start : start + WIDE] = g1[i * NY + j]
-    send(c0, proj.at[ours], send_sem.at[3], recv_sem.at[3], sibling)
+    @pl.when(mine < OWNERS)
+    def _():
+        r1[mine] = half[
+            sixteen(mine // GROUPS), pl.ds(pl.multiple_of(lax.rem(mine, GROUPS) * STEP, STEP), STEP)
+        ]
+        wait_bytes(r1.at[pl.ds(0, NX * NY - 1)], recv_sem.at[0])
+        total = r1[0].astype(F32)
+        for i in range(1, NX * NY):
+            total = total + r1[i].astype(F32)
+        z1[z] = total.astype(BF16)
+        for dz in ZS:
+            send(z1.at[z], z1.at[z], send_sem.at[1], recv_sem.at[1], z_peer(dz))
+        wait_bytes(z1.at[pl.ds(0, NZ - 1)], recv_sem.at[1])
+        total = z1[0].astype(F32)
+        for i in range(1, NZ):
+            total = total + z1[i].astype(F32)
+        g1[mine] = total.astype(BF16)
+        for dx, dy in XY:
+            send(g1.at[mine], g1.at[mine], send_sem.at[2], recv_sem.at[2], xy_peer(dx, dy))
+        wait_bytes(g1.at[pl.ds(0, OWNERS - 1)], recv_sem.at[2])
+
+    @pl.when(mine >= OWNERS)
+    def _():
+        wait_bytes(g1, recv_sem.at[2])
+
+    for owner in range(OWNERS):
+        row, column = owner // GROUPS * 16, owner % GROUPS * STEP
+        left[row : row + 16, column : column + STEP] = g1[owner]
+    send(left, proj.at[ours], send_sem.at[3], recv_sem.at[3], sibling)
     wait_bytes(twin, recv_sem.at[4])
-    left = c0[...]
-    high = left.astype(BF16)
-    low = (left - high.astype(F32)).astype(BF16)
-    stack = jnp.concatenate([high, low], axis=0)
     for h in range(2):
         columns = pl.ds(h * HALF, HALF)
-        both = jnp.dot(stack, merged[:, columns], preferred_element_type=F32)
-        both = both + jnp.dot(stack, twin[:, columns], preferred_element_type=F32)
-        fb[:, columns] = (both[:32] + both[32:]).astype(BF16)
+        both = jnp.dot(left[...], merged[:, columns], preferred_element_type=F32)
+        both = both + jnp.dot(left[...], twin[:, columns], preferred_element_type=F32)
+        fb[:, columns] = both.astype(BF16)
         for dy in (2, 1, 3):
             ty = lax.rem(y + dy, NY)
 
@@ -232,12 +234,10 @@
 
     fr[y] = fb[sixteen(y // 2), lane_half(lax.rem(y, 2))]
 
-    proj[ours, :] = left
-    wait_bytes(half, recv_sem.at[3])
-    left = proj[...]
+    proj[ours, :] = left[...]
+    wait_bytes(left, recv_sem.at[3])
     gram = lax.dot_general(
-        left, left, (((1,), (1,)), ((), ())),
-        precision=lax.Precision.HIGHEST, preferred_element_type=F32,
+        proj[...], proj[...], (((1,), (1,)), ((), ())), preferred_element_type=F32
     )
     eye = (
         lax.broadcasted_iota(jnp.int32, (RANK, RANK), 0)
@@ -272,16 +272,14 @@
     eliminated = eliminate(46, RANK, work[...])
     diagonal = jnp.sum(eliminated[:, :RANK] * eye, axis=1, keepdims=True)
     inverse = eliminated[:, RANK:] * lax.rsqrt(diagonal)
-    basis_out[...] = jnp.dot(
-        inverse, proj[...], precision=lax.Precision.HIGHEST, preferred_element_type=F32
-    ).astype(BF16)
-
-    wait_bytes(landed, recv_sem.at[7])
     high = inverse.astype(BF16)
     low = (inverse - high.astype(F32)).astype(BF16)
-    both = jnp.dot(
-        jnp.concatenate([high, low], axis=0), fs[...], preferred_element_type=F32
-    )
+    split = jnp.concatenate([high, low], axis=0)
+    both = jnp.dot(split, proj[...], preferred_element_type=F32)
+    basis_out[...] = (both[:RANK] + both[RANK:]).astype(BF16)
+
+    wait_bytes(landed, recv_sem.at[7])
+    both = jnp.dot(split, fs[...], preferred_element_type=F32)
     q = (both[:RANK] + both[RANK:]) * (1.0 / REPLICAS)
     q_new[...] = q
     q_low[...] = q.astype(BF16)
@@ -289,10 +287,17 @@
 
     for i, r in enumerate(range(0, ROWS, STEP)):
         wait_bytes(c0.at[:, pl.ds(r, STEP)], core_send.at[i])
-    wait_bytes(r1, send_sem.at[0])
-    wait_bytes(z1.at[pl.ds(0, NZ - 1)], send_sem.at[1])
-    wait_bytes(r1, send_sem.at[2])
-    wait_bytes(half, send_sem.at[3])
+    @pl.when(mine < OWNERS)
+    def _():
+        wait_bytes(r1.at[pl.ds(0, OWNERS - 1)], send_sem.at[0])
+        wait_bytes(z1.at[pl.ds(0, NZ - 1)], send_sem.at[1])
+        wait_bytes(r1.at[pl.ds(0, NX * NY - 1)], send_sem.at[2])
+
+    @pl.when(mine >= OWNERS)
+    def _():
+        wait_bytes(r1.at[pl.ds(0, OWNERS)], send_sem.at[0])
+
+    wait_bytes(left, send_sem.at[3])
     wait_bytes(twin, send_sem.at[4])
     wait_bytes(fr.at[pl.ds(0, NY - 1)], send_sem.at[5])
     wait_bytes(z2.at[pl.ds(0, NZ - 1)], send_sem.at[6])
@@ -342,20 +347,21 @@
             pltpu.VMEM((TOK, 2 * RANK), BF16),
             pltpu.VMEM((RANK, ROWS), F32),
             pltpu.VMEM((RANK // 2, ROWS), F32),
-            pltpu.VMEM((RANK // 2, ROWS), F32),
+            pltpu.VMEM((RANK // 2, ROWS), BF16),
             pltpu.VMEM((ROWS, COLS), BF16),
-            pltpu.VMEM((NX * NY - 1, 8, WIDE), F32),
-            pltpu.VMEM((NZ, 8, WIDE), F32),
-            pltpu.VMEM((NX * NY, 8, WIDE), F32),
-            pltpu.VMEM((RANK, ROWS), F32),
+            pltpu.VMEM((NX * NY, 16, STEP), BF16),
+            pltpu.VMEM((NZ, 16, STEP), BF16),
+            pltpu.VMEM((OWNERS, 16, STEP), BF16),
+            pltpu.VMEM((RANK // 2, ROWS), BF16),
+            pltpu.VMEM((RANK, ROWS), BF16),
             pltpu.VMEM((RANK, 2 * RANK), F32),
             pltpu.VMEM((RANK // 2, COLS), BF16),
             pltpu.VMEM((NY, 16, HALF), BF16),
             pltpu.VMEM((RANK, COLS), BF16),
             pltpu.VMEM((NZ, 16, HALF), BF16),
-            pltpu.SemaphoreType.DMA((5,)),
-            pltpu.SemaphoreType.DMA((5,)),
-            pltpu.SemaphoreType.DMA((5,)),
+            pltpu.SemaphoreType.DMA((6,)),
+            pltpu.SemaphoreType.DMA((GROUPS,)),
+            pltpu.SemaphoreType.DMA((GROUPS,)),
             pltpu.SemaphoreType.DMA((8,)),
             pltpu.SemaphoreType.DMA((8,)),
         ],

time: 46.5 us -> 44 us (0.946)
  Pallas kernels: 45.8 us -> 43.3 us
    pallas_call x1, Pallas kernels: 43.7 us -> 41.2 us  [body(): pl.pallas_call(sum_kernel, out_shape=(pltpu.VMEM((ROWS, COLS), BF16), plt...]
where the time goes in v4:
time: 44 us; the launch traced here: 43.9 us
  Pallas kernels  43.3 us (98%)
  between operations  0.64 us (1%)
    pallas_call x1, Pallas kernels, body(): pl.pallas_call(sum_kernel, out_shape=(pltpu.VMEM((ROWS, COLS), BF16), plt...  41.2 us
    pallas_call x1, Pallas kernels, body(): pl.pallas_call(update_kernel, in_specs=[inside] * 4, out_specs=(anywhere,...  2.1 us

profile of v4, /device:TPU:1, one launch (start us, length us, event | category | flops | bytes accessed | tf_op | source)
XLA Modules:
  0.0 43.9 jit_solution(4325157122865836527)
XLA Ops:
  0.6 41.2 %sums.1 = (bf16[1280,1280]{1,0:T(8,128)(2,1)S(1)}, f32[64,1280]{1,0:T(8,128)S(1)}, bf16[64,1280]{1,0:T(8,128)(2,1)S(1)}, bf16[64,1280]{1,0:T(8,128)(2,1)S(1)}) custom-call(bf16[1024,1280]{1,0:T(8,128)(2,1)} %acts.1, bf16[1024,1280]{1,0:T(8,128)(2,1)} %cot.1, bf16[1280,1280]{1,0:T(8,128)(2,1)} %err.1, bf16[64,1280]{1,0:T(8,128)(2,1)} %q_ref.1), custom_call_target="tpu_custom_call" | custom-call | tf_op jit(solution)/shard_map/sums/pallas_call | solution.py:332
  41.8 2.1 %update.1 = (bf16[1280,1280]{1,0:T(8,128)(2,1)}, f32[64,1280]{1,0:T(8,128)}) custom-call(bf16[1280,1280]{1,0:T(8,128)(2,1)S(1)} %get-tuple-element.6.merged, f32[64,1280]{1,0:T(8,128)S(1)} %get-tuple-element.7.q_in, bf16[64,1280]{1,0:T(8,128)(2,1)S(1)} %get-tuple-element.8.q_low, bf16[64,1280]{1,0:T(8,128)(2,1)S(1)} %get-tuple-element.9.basis), custom_call_target="tpu_custom_call" | custom-call | tf_op jit(solution)/shard_map/update/pallas_call | solution.py:374

commit v5 on v4

--- a/solution.py
+++ b/solution.py
@@ -45,6 +45,10 @@
     key=lambda d: -(hops(d[0], NX) + hops(d[1], NY)),
 )
 ZS = sorted(range(1, NZ), key=lambda d: -hops(d, NZ))
+
+
+def place(owner):
+    return owner * 8 // 5
 
 
 def sixteen(i):
@@ -165,32 +169,38 @@
             part.at[theirs, columns], c0.at[:, columns], core_send.at[i], core_recv.at[i], sibling
         )
     mine = x * NY + y
+    held = (mine * 5 + 7) // 8
+    owns = place(held) == mine
+    foreign = place(held) != mine
     for i in range(GROUPS):
         columns = pl.ds(i * STEP, STEP)
         wait_bytes(c0.at[:, columns], core_recv.at[i])
         half[:, columns] = (part[ours, columns] + c0[:, columns]).astype(BF16)
         for owner in (i, GROUPS + i):
 
-            @pl.when(mine != owner)
+            @pl.when(mine != place(owner))
             def _():
                 send(
                     half.at[pl.ds(owner // GROUPS * 16, 16), columns], r1.at[mine],
-                    send_sem.at[0], recv_sem.at[0], device(owner // NY, owner % NY, z, c),
+                    send_sem.at[0], recv_sem.at[0], device(place(owner) // NY, place(owner) % NY, z, c),
                 )
 
-    for r in range(0, ROWS, STEP):
-        grad = lax.dot_general(
-            acts_v[:, r : r + STEP], cot_v[...], (((0,), (0,)), ((), ())),
-            preferred_element_type=F32,
-        )
-        merged[r : r + STEP, :] = (grad + err_v[r : r + STEP, :].astype(F32)).astype(BF16)
-        block = pl.ds(r, STEP)
-        send(merged.at[block], twin.at[block], send_sem.at[4], recv_sem.at[4], sibling)
-
-    @pl.when(mine < OWNERS)
+    def merge(first, last):
+        for r in range(first, last, STEP):
+            grad = lax.dot_general(
+                acts_v[:, r : r + STEP], cot_v[...], (((0,), (0,)), ((), ())),
+                preferred_element_type=F32,
+            )
+            merged[r : r + STEP, :] = (grad + err_v[r : r + STEP, :].astype(F32)).astype(BF16)
+            rows = pl.ds(r, STEP)
+            send(merged.at[rows], twin.at[rows], send_sem.at[4], recv_sem.at[4], sibling)
+
+    merge(0, 2 * STEP)
+
+    @pl.when(owns)
     def _():
         r1[mine] = half[
-            sixteen(mine // GROUPS), pl.ds(pl.multiple_of(lax.rem(mine, GROUPS) * STEP, STEP), STEP)
+            sixteen(held // GROUPS), pl.ds(pl.multiple_of(lax.rem(held, GROUPS) * STEP, STEP), STEP)
         ]
         wait_bytes(r1.at[pl.ds(0, NX * NY - 1)], recv_sem.at[0])
         total = r1[0].astype(F32)
@@ -199,16 +209,21 @@
         z1[z] = total.astype(BF16)
         for dz in ZS:
             send(z1.at[z], z1.at[z], send_sem.at[1], recv_sem.at[1], z_peer(dz))
+
+    merge(2 * STEP, ROWS)
+
+    @pl.when(owns)
+    def _():
         wait_bytes(z1.at[pl.ds(0, NZ - 1)], recv_sem.at[1])
         total = z1[0].astype(F32)
         for i in range(1, NZ):
             total = total + z1[i].astype(F32)
-        g1[mine] = total.astype(BF16)
+        g1[held] = total.astype(BF16)
         for dx, dy in XY:
-            send(g1.at[mine], g1.at[mine], send_sem.at[2], recv_sem.at[2], xy_peer(dx, dy))
+            send(g1.at[held], g1.at[held], send_sem.at[2], recv_sem.at[2], xy_peer(dx, dy))
         wait_bytes(g1.at[pl.ds(0, OWNERS - 1)], recv_sem.at[2])
 
-    @pl.when(mine >= OWNERS)
+    @pl.when(foreign)
     def _():
         wait_bytes(g1, recv_sem.at[2])
 
@@ -287,13 +302,13 @@
 
     for i, r in enumerate(range(0, ROWS, STEP)):
         wait_bytes(c0.at[:, pl.ds(r, STEP)], core_send.at[i])
-    @pl.when(mine < OWNERS)
+    @pl.when(owns)
     def _():
         wait_bytes(r1.at[pl.ds(0, OWNERS - 1)], send_sem.at[0])
         wait_bytes(z1.at[pl.ds(0, NZ - 1)], send_sem.at[1])
         wait_bytes(r1.at[pl.ds(0, NX * NY - 1)], send_sem.at[2])
 
-    @pl.when(mine >= OWNERS)
+    @pl.when(foreign)
     def _():
         wait_bytes(r1.at[pl.ds(0, OWNERS)], send_sem.at[0])
 

time: 44 us -> 43.6 us (level)
  Pallas kernels: 43.3 us -> 42.8 us
where the time goes in v5:
time: 43.6 us; the launch traced here: 43.5 us
  Pallas kernels  42.8 us (98%)
  between operations  0.64 us (1%)
    pallas_call x1, Pallas kernels, body(): pl.pallas_call(sum_kernel, out_shape=(pltpu.VMEM((ROWS, COLS), BF16), plt...  40.7 us
    pallas_call x1, Pallas kernels, body(): pl.pallas_call(update_kernel, in_specs=[inside] * 4, out_specs=(anywhere,...  2.11 us

profile of v5, /device:TPU:1, one launch (start us, length us, event | category | flops | bytes accessed | tf_op | source)
XLA Modules:
  0.0 43.5 jit_solution(5555999195295363194)
XLA Ops:
  0.6 40.7 %sums.1 = (bf16[1280,1280]{1,0:T(8,128)(2,1)S(1)}, f32[64,1280]{1,0:T(8,128)S(1)}, bf16[64,1280]{1,0:T(8,128)(2,1)S(1)}, bf16[64,1280]{1,0:T(8,128)(2,1)S(1)}) custom-call(bf16[1024,1280]{1,0:T(8,128)(2,1)} %acts.1, bf16[1024,1280]{1,0:T(8,128)(2,1)} %cot.1, bf16[1280,1280]{1,0:T(8,128)(2,1)} %err.1, bf16[64,1280]{1,0:T(8,128)(2,1)} %q_ref.1), custom_call_target="tpu_custom_call" | custom-call | tf_op jit(solution)/shard_map/sums/pallas_call | solution.py:347
  41.4 2.1 %update.1 = (bf16[1280,1280]{1,0:T(8,128)(2,1)}, f32[64,1280]{1,0:T(8,128)}) custom-call(bf16[1280,1280]{1,0:T(8,128)(2,1)S(1)} %get-tuple-element.6.merged, f32[64,1280]{1,0:T(8,128)S(1)} %get-tuple-element.7.q_in, bf16[64,1280]{1,0:T(8,128)(2,1)S(1)} %get-tuple-element.8.q_low, bf16[64,1280]{1,0:T(8,128)(2,1)S(1)} %get-tuple-element.9.basis), custom_call_target="tpu_custom_call" | custom-call | tf_op jit(solution)/shard_map/update/pallas_call | solution.py:389

commit v6 on v5

--- a/solution.py
+++ b/solution.py
@@ -79,9 +79,9 @@
     acts, cot, err, q_ref,
     merged, q_new, q_low, basis_out,
     acts_v, cot_v, err_v, q_v, weight, part,
-    c0, half, twin, r1, z1, g1, left, proj, work,
+    half, twin, r1, z1, g1, left, proj, work,
     fb, fr, fs, z2,
-    in_sem, core_send, core_recv, send_sem, recv_sem,
+    in_sem, send_sem, recv_sem,
 ):
     dp = lax.axis_index("dp")
     x = lax.axis_index("tensor")
@@ -130,8 +130,8 @@
     for dz in ZS:
         greet(z_peer(dz))
     greet(sibling)
-    for dy in range(1, NY):
-        greet(device(x, lax.rem(y + dy, NY), z, other))
+    for dx, dy in XY:
+        greet(device(lax.rem(x + dx, NX), lax.rem(y + dy, NY), z, other))
 
     next_copy()
     for r in range(0, TOK, 512):
@@ -149,7 +149,10 @@
             preferred_element_type=F32,
         )
     ours = pl.ds(pl.multiple_of(c * 32, 32), 32)
-    theirs = pl.ds(pl.multiple_of(other * 32, 32), 32)
+    mine = x * NY + y
+    held = (mine * 5 + 7) // 8
+    owns = place(held) == mine
+    foreign = place(held) != mine
     next_copy()
     both = lax.dot_general(
         weight[:512, :], acts_v[:512, :], (((0,), (0,)), ((), ())), preferred_element_type=F32
@@ -163,27 +166,19 @@
         )
         part[:, r : r + STEP] += both[:RANK] + both[RANK:]
         if i == 0:
-            pl.semaphore_wait(barrier, len(XY) + len(ZS) + NY)
+            pl.semaphore_wait(barrier, 2 * len(XY) + len(ZS) + 1)
         columns = pl.ds(r, STEP)
-        send(
-            part.at[theirs, columns], c0.at[:, columns], core_send.at[i], core_recv.at[i], sibling
-        )
-    mine = x * NY + y
-    held = (mine * 5 + 7) // 8
-    owns = place(held) == mine
-    foreign = place(held) != mine
-    for i in range(GROUPS):
-        columns = pl.ds(i * STEP, STEP)
-        wait_bytes(c0.at[:, columns], core_recv.at[i])
-        half[:, columns] = (part[ours, columns] + c0[:, columns]).astype(BF16)
-        for owner in (i, GROUPS + i):
-
-            @pl.when(mine != place(owner))
-            def _():
-                send(
-                    half.at[pl.ds(owner // GROUPS * 16, 16), columns], r1.at[mine],
-                    send_sem.at[0], recv_sem.at[0], device(place(owner) // NY, place(owner) % NY, z, c),
-                )
+        half[:, columns] = part[:, columns].astype(BF16)
+        for core in range(2):
+            for owner in (i, GROUPS + i):
+
+                @pl.when(jnp.logical_or(mine != place(owner), c != core))
+                def _():
+                    send(
+                        half.at[pl.ds(core * 32 + owner // GROUPS * 16, 16), columns],
+                        r1.at[mine * 2 + c], send_sem.at[0], recv_sem.at[0],
+                        device(place(owner) // NY, place(owner) % NY, z, core),
+                    )
 
     def merge(first, last):
         for r in range(first, last, STEP):
@@ -199,12 +194,12 @@
 
     @pl.when(owns)
     def _():
-        r1[mine] = half[
-            sixteen(held // GROUPS), pl.ds(pl.multiple_of(lax.rem(held, GROUPS) * STEP, STEP), STEP)
+        r1[mine * 2 + c] = half[
+            sixteen(2 * c + held // GROUPS), pl.ds(pl.multiple_of(lax.rem(held, GROUPS) * STEP, STEP), STEP)
         ]
-        wait_bytes(r1.at[pl.ds(0, NX * NY - 1)], recv_sem.at[0])
+        wait_bytes(r1.at[pl.ds(0, 2 * NX * NY - 1)], recv_sem.at[0])
         total = r1[0].astype(F32)
-        for i in range(1, NX * NY):
+        for i in range(1, 2 * NX * NY):
             total = total + r1[i].astype(F32)
         z1[z] = total.astype(BF16)
         for dz in ZS:
@@ -300,17 +295,15 @@
     q_low[...] = q.astype(BF16)
 
 
-    for i, r in enumerate(range(0, ROWS, STEP)):
-        wait_bytes(c0.at[:, pl.ds(r, STEP)], core_send.at[i])
     @pl.when(owns)
     def _():
-        wait_bytes(r1.at[pl.ds(0, OWNERS - 1)], send_sem.at[0])
+        wait_bytes(r1.at[pl.ds(0, 2 * OWNERS - 1)], send_sem.at[0])
         wait_bytes(z1.at[pl.ds(0, NZ - 1)], send_sem.at[1])
         wait_bytes(r1.at[pl.ds(0, NX * NY - 1)], send_sem.at[2])
 
     @pl.when(foreign)
     def _():
-        wait_bytes(r1.at[pl.ds(0, OWNERS)], send_sem.at[0])
+        wait_bytes(r1.at[pl.ds(0, 2 * OWNERS)], send_sem.at[0])
 
     wait_bytes(left, send_sem.at[3])
     wait_bytes(twin, send_sem.at[4])
@@ -361,10 +354,9 @@
             pltpu.VMEM((RANK, COLS), BF16),
             pltpu.VMEM((TOK, 2 * RANK), BF16),
             pltpu.VMEM((RANK, ROWS), F32),
-            pltpu.VMEM((RANK // 2, ROWS), F32),
-            pltpu.VMEM((RANK // 2, ROWS), BF16),
+            pltpu.VMEM((RANK, ROWS), BF16),
             pltpu.VMEM((ROWS, COLS), BF16),
-            pltpu.VMEM((NX * NY, 16, STEP), BF16),
+            pltpu.VMEM((2 * NX * NY, 16, STEP), BF16),
             pltpu.VMEM((NZ, 16, STEP), BF16),
             pltpu.VMEM((OWNERS, 16, STEP), BF16),
             pltpu.VMEM((RANK // 2, ROWS), BF16),
@@ -375,8 +367,6 @@
             pltpu.VMEM((RANK, COLS), BF16),
             pltpu.VMEM((NZ, 16, HALF), BF16),
             pltpu.SemaphoreType.DMA((6,)),
-            pltpu.SemaphoreType.DMA((GROUPS,)),
-            pltpu.SemaphoreType.DMA((GROUPS,)),
             pltpu.SemaphoreType.DMA((8,)),
             pltpu.SemaphoreType.DMA((8,)),
         ],

time: 43.6 us -> 43.4 us (level)
  no operation moved by 1% of the time
where the time goes in v6:
time: 43.4 us; the launch traced here: 43.3 us
  Pallas kernels  42.7 us (98%)
  between operations  0.64 us (1%)
    pallas_call x1, Pallas kernels, body(): pl.pallas_call(sum_kernel, out_shape=(pltpu.VMEM((ROWS, COLS), BF16), plt...  40.6 us
    pallas_call x1, Pallas kernels, body(): pl.pallas_call(update_kernel, in_specs=[inside] * 4, out_specs=(anywhere,...  2.11 us

profile of v6, /device:TPU:1, one launch (start us, length us, event | category | flops | bytes accessed | tf_op | source)
XLA Modules:
  0.0 43.3 jit_solution(7610707875432755269)
XLA Ops:
  0.6 40.6 %sums.1 = (bf16[1280,1280]{1,0:T(8,128)(2,1)S(1)}, f32[64,1280]{1,0:T(8,128)S(1)}, bf16[64,1280]{1,0:T(8,128)(2,1)S(1)}, bf16[64,1280]{1,0:T(8,128)(2,1)S(1)}) custom-call(bf16[1024,1280]{1,0:T(8,128)(2,1)} %acts.1, bf16[1024,1280]{1,0:T(8,128)(2,1)} %cot.1, bf16[1280,1280]{1,0:T(8,128)(2,1)} %err.1, bf16[64,1280]{1,0:T(8,128)(2,1)} %q_ref.1), custom_call_target="tpu_custom_call" | custom-call | tf_op jit(solution)/shard_map/sums/pallas_call | solution.py:340
  41.2 2.1 %update.1 = (bf16[1280,1280]{1,0:T(8,128)(2,1)}, f32[64,1280]{1,0:T(8,128)}) custom-call(bf16[1280,1280]{1,0:T(8,128)(2,1)S(1)} %get-tuple-element.6.merged, f32[64,1280]{1,0:T(8,128)S(1)} %get-tuple-element.7.q_in, bf16[64,1280]{1,0:T(8,128)(2,1)S(1)} %get-tuple-element.8.q_low, bf16[64,1280]{1,0:T(8,128)(2,1)S(1)} %get-tuple-element.9.basis), custom_call_target="tpu_custom_call" | custom-call | tf_op jit(solution)/shard_map/update/pallas_call | solution.py:379
